TPU v7x, 256 devices: a whole 4x4x8 slice. The times are simulated.
256 devices in a mesh: feat: 16 (over x_hi, z), ex: 16 (over y, x_lo, core).
Axes of the slice: x: 4 (x_hi: 2, x_lo: 2; x = x_hi * 2 + x_lo), y: 4, z: 8, core: 2. Of those that a mesh axis runs over, the one named last changes fastest.
Arguments:
- queries: bfloat16 [2048, 32768], P('ex', 'feat'), may hold values from -6 to 6
- train_grads: bfloat16 [16384, 32768], P('ex', 'feat'), may hold values from -0.03125 to 0.03125
Outputs:
- scores: float32 [2048, 16384], P('feat', 'ex')
All inputs are finite; a program needn't handle non-finite values.
Results may differ from a plain program's by a relative error of at most 0.0003.
Values may be sent and summed in bfloat16 or wider, within the bound.
No kernel may reach another device: no remote copies, remote signals or barrier semaphores. Data moves between devices by JAX's collectives and lax.ppermute only.
A program may use at most 64 MiB of HBM per device.

v0:
```python
import jax
import jax.numpy as jnp
from jax import lax
from jax.sharding import PartitionSpec as P


def shifted(block, axis, distance):
    devices = range(lax.axis_size(axis))
    route = [((i - distance) % len(devices), i) for i in devices]
    return lax.ppermute(block, axis, route)


def block_scores(block, train_grads):
    return lax.dot_general(
        block, train_grads, (((1,), (1,)), ((), ())), preferred_element_type=jnp.float32
    )


def place_rows(total, block, train_grads, first):
    part = block_scores(block, train_grads)
    return lax.dynamic_update_slice(total, part, (first, jnp.int32(0)))


def on_device(queries, train_grads):
    count = lax.axis_size("ex")
    myself = lax.axis_index("ex")
    qrows = queries.shape[0]
    total = jnp.zeros((count * qrows, train_grads.shape[0]), jnp.float32)
    total = place_rows(total, queries, train_grads, myself * qrows)

    def step_one(turn, carry):
        acc, held = carry
        held = shifted(held, "ex", 1)
        anchor = (myself - turn) % count
        return (place_rows(acc, held, train_grads, anchor * qrows), held)

    total, _ = lax.fori_loop(1, count, step_one, (total, queries))
    return lax.psum_scatter(total, "feat", scatter_dimension=0, tiled=True)


def solution(mesh):
    return jax.shard_map(
        on_device,
        mesh=mesh,
        in_specs=(P("ex", "feat"), P("ex", "feat")),
        out_specs=P("feat", "ex"),
        check_vma=False,
    )
```

profile of v0, /device:TPU:8, one launch (start us, length us, event | category | flops | bytes accessed | tf_op | source)
XLA Modules:
  0.0 477.9 jit_solution(2552575884843100843)
XLA Ops:
  14.5 211.0 %while.17 = (s32[]{:T(128)}, f32[2048,1024]{1,0:T(8,128)}, bf16[128,2048]{1,0:T(8,128)(2,1)S(1)}, bf16[1024,2048]{1,0:T(8,128)(2,1)}, s32[]{:T(128)}, /*index=5*...) while((s32[]{:T(128)}, f32[2048,1024]{1,0:T(8,128)}, ...), condition=%wide.region_1.2_spmd, body=%wide.region_0.1_spmd.sunk | while | flops 536870912 | bytes 8388928 | solution.py:37
  14.5 9.5 %collective-permute-done = bf16[128,2048]{1,0:T(8,128)(2,1)S(1)} collective-permute-done((bf16[128,2048]{1,0:T(8,128)(2,1)S(1)}, bf16[128,2048]{1,0:T(8,128)(2,1)S(1)}, u32[]{:S(2)}, u32[]{:S(2)}) %collective-permute-start) | collective-permute-done | bytes 524320 | tf_op jit(solution)/shard_map/while/body/eval_jaxpr/ppermute | solution.py:10
  24.1 4.5 convolution_dynamic-update-slice_fusion.3
  28.6 9.5 %collective-permute-done = bf16[128,2048]{1,0:T(8,128)(2,1)S(1)} collective-permute-done((bf16[128,2048]{1,0:T(8,128)(2,1)S(1)}, bf16[128,2048]{1,0:T(8,128)(2,1)S(1)}, u32[]{:S(2)}, u32[]{:S(2)}) %collective-permute-start) | collective-permute-done | bytes 524320 | tf_op jit(solution)/shard_map/while/body/eval_jaxpr/ppermute | solution.py:10
  38.1 4.5 convolution_dynamic-update-slice_fusion.3
  42.6 9.5 %collective-permute-done = bf16[128,2048]{1,0:T(8,128)(2,1)S(1)} collective-permute-done((bf16[128,2048]{1,0:T(8,128)(2,1)S(1)}, bf16[128,2048]{1,0:T(8,128)(2,1)S(1)}, u32[]{:S(2)}, u32[]{:S(2)}) %collective-permute-start) | collective-permute-done | bytes 524320 | tf_op jit(solution)/shard_map/while/body/eval_jaxpr/ppermute | solution.py:10
  52.2 4.5 convolution_dynamic-update-slice_fusion.3
  56.7 9.5 %collective-permute-done = bf16[128,2048]{1,0:T(8,128)(2,1)S(1)} collective-permute-done((bf16[128,2048]{1,0:T(8,128)(2,1)S(1)}, bf16[128,2048]{1,0:T(8,128)(2,1)S(1)}, u32[]{:S(2)}, u32[]{:S(2)}) %collective-permute-start) | collective-permute-done | bytes 524320 | tf_op jit(solution)/shard_map/while/body/eval_jaxpr/ppermute | solution.py:10
  66.2 4.5 convolution_dynamic-update-slice_fusion.3
  70.7 9.5 %collective-permute-done = bf16[128,2048]{1,0:T(8,128)(2,1)S(1)} collective-permute-done((bf16[128,2048]{1,0:T(8,128)(2,1)S(1)}, bf16[128,2048]{1,0:T(8,128)(2,1)S(1)}, u32[]{:S(2)}, u32[]{:S(2)}) %collective-permute-start) | collective-permute-done | bytes 524320 | tf_op jit(solution)/shard_map/while/body/eval_jaxpr/ppermute | solution.py:10
  80.3 4.5 convolution_dynamic-update-slice_fusion.3
  84.8 9.5 %collective-permute-done = bf16[128,2048]{1,0:T(8,128)(2,1)S(1)} collective-permute-done((bf16[128,2048]{1,0:T(8,128)(2,1)S(1)}, bf16[128,2048]{1,0:T(8,128)(2,1)S(1)}, u32[]{:S(2)}, u32[]{:S(2)}) %collective-permute-start) | collective-permute-done | bytes 524320 | tf_op jit(solution)/shard_map/while/body/eval_jaxpr/ppermute | solution.py:10
  94.4 4.5 convolution_dynamic-update-slice_fusion.3
  98.9 9.5 %collective-permute-done = bf16[128,2048]{1,0:T(8,128)(2,1)S(1)} collective-permute-done((bf16[128,2048]{1,0:T(8,128)(2,1)S(1)}, bf16[128,2048]{1,0:T(8,128)(2,1)S(1)}, u32[]{:S(2)}, u32[]{:S(2)}) %collective-permute-start) | collective-permute-done | bytes 524320 | tf_op jit(solution)/shard_map/while/body/eval_jaxpr/ppermute | solution.py:10
  108.4 4.5 convolution_dynamic-update-slice_fusion.3
  113.0 9.5 %collective-permute-done = bf16[128,2048]{1,0:T(8,128)(2,1)S(1)} collective-permute-done((bf16[128,2048]{1,0:T(8,128)(2,1)S(1)}, bf16[128,2048]{1,0:T(8,128)(2,1)S(1)}, u32[]{:S(2)}, u32[]{:S(2)}) %collective-permute-start) | collective-permute-done | bytes 524320 | tf_op jit(solution)/shard_map/while/body/eval_jaxpr/ppermute | solution.py:10
  122.5 4.5 convolution_dynamic-update-slice_fusion.3
  127.0 9.5 %collective-permute-done = bf16[128,2048]{1,0:T(8,128)(2,1)S(1)} collective-permute-done((bf16[128,2048]{1,0:T(8,128)(2,1)S(1)}, bf16[128,2048]{1,0:T(8,128)(2,1)S(1)}, u32[]{:S(2)}, u32[]{:S(2)}) %collective-permute-start) | collective-permute-done | bytes 524320 | tf_op jit(solution)/shard_map/while/body/eval_jaxpr/ppermute | solution.py:10
  136.6 4.5 convolution_dynamic-update-slice_fusion.3
  141.1 9.5 %collective-permute-done = bf16[128,2048]{1,0:T(8,128)(2,1)S(1)} collective-permute-done((bf16[128,2048]{1,0:T(8,128)(2,1)S(1)}, bf16[128,2048]{1,0:T(8,128)(2,1)S(1)}, u32[]{:S(2)}, u32[]{:S(2)}) %collective-permute-start) | collective-permute-done | bytes 524320 | tf_op jit(solution)/shard_map/while/body/eval_jaxpr/ppermute | solution.py:10
  150.6 4.5 convolution_dynamic-update-slice_fusion.3
  155.2 9.5 %collective-permute-done = bf16[128,2048]{1,0:T(8,128)(2,1)S(1)} collective-permute-done((bf16[128,2048]{1,0:T(8,128)(2,1)S(1)}, bf16[128,2048]{1,0:T(8,128)(2,1)S(1)}, u32[]{:S(2)}, u32[]{:S(2)}) %collective-permute-start) | collective-permute-done | bytes 524320 | tf_op jit(solution)/shard_map/while/body/eval_jaxpr/ppermute | solution.py:10
  164.7 4.5 convolution_dynamic-update-slice_fusion.3
  169.3 9.5 %collective-permute-done = bf16[128,2048]{1,0:T(8,128)(2,1)S(1)} collective-permute-done((bf16[128,2048]{1,0:T(8,128)(2,1)S(1)}, bf16[128,2048]{1,0:T(8,128)(2,1)S(1)}, u32[]{:S(2)}, u32[]{:S(2)}) %collective-permute-start) | collective-permute-done | bytes 524320 | tf_op jit(solution)/shard_map/while/body/eval_jaxpr/ppermute | solution.py:10
  178.8 4.5 convolution_dynamic-update-slice_fusion.3
  183.3 9.5 %collective-permute-done = bf16[128,2048]{1,0:T(8,128)(2,1)S(1)} collective-permute-done((bf16[128,2048]{1,0:T(8,128)(2,1)S(1)}, bf16[128,2048]{1,0:T(8,128)(2,1)S(1)}, u32[]{:S(2)}, u32[]{:S(2)}) %collective-permute-start) | collective-permute-done | bytes 524320 | tf_op jit(solution)/shard_map/while/body/eval_jaxpr/ppermute | solution.py:10
  192.9 4.5 convolution_dynamic-update-slice_fusion.3
  197.4 9.5 %collective-permute-done = bf16[128,2048]{1,0:T(8,128)(2,1)S(1)} collective-permute-done((bf16[128,2048]{1,0:T(8,128)(2,1)S(1)}, bf16[128,2048]{1,0:T(8,128)(2,1)S(1)}, u32[]{:S(2)}, u32[]{:S(2)}) %collective-permute-start) | collective-permute-done | bytes 524320 | tf_op jit(solution)/shard_map/while/body/eval_jaxpr/ppermute | solution.py:10
  206.9 4.5 convolution_dynamic-update-slice_fusion.3
  211.4 9.5 %collective-permute-done = bf16[128,2048]{1,0:T(8,128)(2,1)S(1)} collective-permute-done((bf16[128,2048]{1,0:T(8,128)(2,1)S(1)}, bf16[128,2048]{1,0:T(8,128)(2,1)S(1)}, u32[]{:S(2)}, u32[]{:S(2)}) %collective-permute-start) | collective-permute-done | bytes 524320 | tf_op jit(solution)/shard_map/while/body/eval_jaxpr/ppermute | solution.py:10
  221.0 4.5 convolution_dynamic-update-slice_fusion.3
  225.5 245.6 %reduce-scatter.2.cloned.1.call-done = f32[128,1024]{1,0:T(8,128)} async-done(((f32[2048,1024]{1,0:T(8,128)}), f32[128,1024]{1,0:T(8,128)}) %reduce-scatter.2.cloned.1.call-update) | async-done | bytes 524304 | tf_op jit(solution)/shard_map/reduce_scatter | solution.py:38
  (39 shorter events, 8.6 us)
Async XLA Ops:
  6.5 464.6 %reduce-scatter.2.cloned.1.call-start = ((), (), s32[]{:S(2)}) async-start(), calls=%async_computation.1 | async-start | bytes 8912896 | tf_op jit(solution)/shard_map/reduce_scatter | solution.py:38
  7.6 2.2 copy-start
  11.3 3.2 copy-start.1
  14.5 9.5 %collective-permute-start = (bf16[128,2048]{1,0:T(8,128)(2,1)S(1)}, bf16[128,2048]{1,0:T(8,128)(2,1)S(1)}, u32[]{:S(2)}, u32[]{:S(2)}) collective-permute-start(bf16[128,2048]{1,0:T(8,128)(2,1)S(1)} %get-tuple-element.193), channel_id=1, source_target_pairs={{15,0},{0,1},{1,2},{2,3},{3,4},{4,5},{5,6},{6,7},{7,8},{8,9},{9,10... | collective-permute-start | bytes 1572872 | tf_op jit(solution)/shard_map/while/body/eval_jaxpr/ppermute | solution.py:10
  28.5 9.5 %collective-permute-start = (bf16[128,2048]{1,0:T(8,128)(2,1)S(1)}, bf16[128,2048]{1,0:T(8,128)(2,1)S(1)}, u32[]{:S(2)}, u32[]{:S(2)}) collective-permute-start(bf16[128,2048]{1,0:T(8,128)(2,1)S(1)} %get-tuple-element.193), channel_id=1, source_target_pairs={{15,0},{0,1},{1,2},{2,3},{3,4},{4,5},{5,6},{6,7},{7,8},{8,9},{9,10... | collective-permute-start | bytes 1572872 | tf_op jit(solution)/shard_map/while/body/eval_jaxpr/ppermute | solution.py:10
  42.6 9.5 %collective-permute-start = (bf16[128,2048]{1,0:T(8,128)(2,1)S(1)}, bf16[128,2048]{1,0:T(8,128)(2,1)S(1)}, u32[]{:S(2)}, u32[]{:S(2)}) collective-permute-start(bf16[128,2048]{1,0:T(8,128)(2,1)S(1)} %get-tuple-element.193), channel_id=1, source_target_pairs={{15,0},{0,1},{1,2},{2,3},{3,4},{4,5},{5,6},{6,7},{7,8},{8,9},{9,10... | collective-permute-start | bytes 1572872 | tf_op jit(solution)/shard_map/while/body/eval_jaxpr/ppermute | solution.py:10
  56.7 9.5 %collective-permute-start = (bf16[128,2048]{1,0:T(8,128)(2,1)S(1)}, bf16[128,2048]{1,0:T(8,128)(2,1)S(1)}, u32[]{:S(2)}, u32[]{:S(2)}) collective-permute-start(bf16[128,2048]{1,0:T(8,128)(2,1)S(1)} %get-tuple-element.193), channel_id=1, source_target_pairs={{15,0},{0,1},{1,2},{2,3},{3,4},{4,5},{5,6},{6,7},{7,8},{8,9},{9,10... | collective-permute-start | bytes 1572872 | tf_op jit(solution)/shard_map/while/body/eval_jaxpr/ppermute | solution.py:10
  70.7 9.5 %collective-permute-start = (bf16[128,2048]{1,0:T(8,128)(2,1)S(1)}, bf16[128,2048]{1,0:T(8,128)(2,1)S(1)}, u32[]{:S(2)}, u32[]{:S(2)}) collective-permute-start(bf16[128,2048]{1,0:T(8,128)(2,1)S(1)} %get-tuple-element.193), channel_id=1, source_target_pairs={{15,0},{0,1},{1,2},{2,3},{3,4},{4,5},{5,6},{6,7},{7,8},{8,9},{9,10... | collective-permute-start | bytes 1572872 | tf_op jit(solution)/shard_map/while/body/eval_jaxpr/ppermute | solution.py:10
  84.8 9.5 %collective-permute-start = (bf16[128,2048]{1,0:T(8,128)(2,1)S(1)}, bf16[128,2048]{1,0:T(8,128)(2,1)S(1)}, u32[]{:S(2)}, u32[]{:S(2)}) collective-permute-start(bf16[128,2048]{1,0:T(8,128)(2,1)S(1)} %get-tuple-element.193), channel_id=1, source_target_pairs={{15,0},{0,1},{1,2},{2,3},{3,4},{4,5},{5,6},{6,7},{7,8},{8,9},{9,10... | collective-permute-start | bytes 1572872 | tf_op jit(solution)/shard_map/while/body/eval_jaxpr/ppermute | solution.py:10
  98.9 9.5 %collective-permute-start = (bf16[128,2048]{1,0:T(8,128)(2,1)S(1)}, bf16[128,2048]{1,0:T(8,128)(2,1)S(1)}, u32[]{:S(2)}, u32[]{:S(2)}) collective-permute-start(bf16[128,2048]{1,0:T(8,128)(2,1)S(1)} %get-tuple-element.193), channel_id=1, source_target_pairs={{15,0},{0,1},{1,2},{2,3},{3,4},{4,5},{5,6},{6,7},{7,8},{8,9},{9,10... | collective-permute-start | bytes 1572872 | tf_op jit(solution)/shard_map/while/body/eval_jaxpr/ppermute | solution.py:10
  113.0 9.5 %collective-permute-start = (bf16[128,2048]{1,0:T(8,128)(2,1)S(1)}, bf16[128,2048]{1,0:T(8,128)(2,1)S(1)}, u32[]{:S(2)}, u32[]{:S(2)}) collective-permute-start(bf16[128,2048]{1,0:T(8,128)(2,1)S(1)} %get-tuple-element.193), channel_id=1, source_target_pairs={{15,0},{0,1},{1,2},{2,3},{3,4},{4,5},{5,6},{6,7},{7,8},{8,9},{9,10... | collective-permute-start | bytes 1572872 | tf_op jit(solution)/shard_map/while/body/eval_jaxpr/ppermute | solution.py:10
  127.0 9.5 %collective-permute-start = (bf16[128,2048]{1,0:T(8,128)(2,1)S(1)}, bf16[128,2048]{1,0:T(8,128)(2,1)S(1)}, u32[]{:S(2)}, u32[]{:S(2)}) collective-permute-start(bf16[128,2048]{1,0:T(8,128)(2,1)S(1)} %get-tuple-element.193), channel_id=1, source_target_pairs={{15,0},{0,1},{1,2},{2,3},{3,4},{4,5},{5,6},{6,7},{7,8},{8,9},{9,10... | collective-permute-start | bytes 1572872 | tf_op jit(solution)/shard_map/while/body/eval_jaxpr/ppermute | solution.py:10
  141.1 9.5 %collective-permute-start = (bf16[128,2048]{1,0:T(8,128)(2,1)S(1)}, bf16[128,2048]{1,0:T(8,128)(2,1)S(1)}, u32[]{:S(2)}, u32[]{:S(2)}) collective-permute-start(bf16[128,2048]{1,0:T(8,128)(2,1)S(1)} %get-tuple-element.193), channel_id=1, source_target_pairs={{15,0},{0,1},{1,2},{2,3},{3,4},{4,5},{5,6},{6,7},{7,8},{8,9},{9,10... | collective-permute-start | bytes 1572872 | tf_op jit(solution)/shard_map/while/body/eval_jaxpr/ppermute | solution.py:10
  155.2 9.5 %collective-permute-start = (bf16[128,2048]{1,0:T(8,128)(2,1)S(1)}, bf16[128,2048]{1,0:T(8,128)(2,1)S(1)}, u32[]{:S(2)}, u32[]{:S(2)}) collective-permute-start(bf16[128,2048]{1,0:T(8,128)(2,1)S(1)} %get-tuple-element.193), channel_id=1, source_target_pairs={{15,0},{0,1},{1,2},{2,3},{3,4},{4,5},{5,6},{6,7},{7,8},{8,9},{9,10... | collective-permute-start | bytes 1572872 | tf_op jit(solution)/shard_map/while/body/eval_jaxpr/ppermute | solution.py:10
  169.3 9.5 %collective-permute-start = (bf16[128,2048]{1,0:T(8,128)(2,1)S(1)}, bf16[128,2048]{1,0:T(8,128)(2,1)S(1)}, u32[]{:S(2)}, u32[]{:S(2)}) collective-permute-start(bf16[128,2048]{1,0:T(8,128)(2,1)S(1)} %get-tuple-element.193), channel_id=1, source_target_pairs={{15,0},{0,1},{1,2},{2,3},{3,4},{4,5},{5,6},{6,7},{7,8},{8,9},{9,10... | collective-permute-start | bytes 1572872 | tf_op jit(solution)/shard_map/while/body/eval_jaxpr/ppermute | solution.py:10
  183.3 9.5 %collective-permute-start = (bf16[128,2048]{1,0:T(8,128)(2,1)S(1)}, bf16[128,2048]{1,0:T(8,128)(2,1)S(1)}, u32[]{:S(2)}, u32[]{:S(2)}) collective-permute-start(bf16[128,2048]{1,0:T(8,128)(2,1)S(1)} %get-tuple-element.193), channel_id=1, source_target_pairs={{15,0},{0,1},{1,2},{2,3},{3,4},{4,5},{5,6},{6,7},{7,8},{8,9},{9,10... | collective-permute-start | bytes 1572872 | tf_op jit(solution)/shard_map/while/body/eval_jaxpr/ppermute | solution.py:10
  197.4 9.5 %collective-permute-start = (bf16[128,2048]{1,0:T(8,128)(2,1)S(1)}, bf16[128,2048]{1,0:T(8,128)(2,1)S(1)}, u32[]{:S(2)}, u32[]{:S(2)}) collective-permute-start(bf16[128,2048]{1,0:T(8,128)(2,1)S(1)} %get-tuple-element.193), channel_id=1, source_target_pairs={{15,0},{0,1},{1,2},{2,3},{3,4},{4,5},{5,6},{6,7},{7,8},{8,9},{9,10... | collective-permute-start | bytes 1572872 | tf_op jit(solution)/shard_map/while/body/eval_jaxpr/ppermute | solution.py:10
  211.4 9.5 %collective-permute-start = (bf16[128,2048]{1,0:T(8,128)(2,1)S(1)}, bf16[128,2048]{1,0:T(8,128)(2,1)S(1)}, u32[]{:S(2)}, u32[]{:S(2)}) collective-permute-start(bf16[128,2048]{1,0:T(8,128)(2,1)S(1)} %get-tuple-element.193), channel_id=1, source_target_pairs={{15,0},{0,1},{1,2},{2,3},{3,4},{4,5},{5,6},{6,7},{7,8},{8,9},{9,10... | collective-permute-start | bytes 1572872 | tf_op jit(solution)/shard_map/while/body/eval_jaxpr/ppermute | solution.py:10
Sparse Core Ops, SparseCore 0:
  225.7 245.3 reduce-scatter.1
where the time goes:
time: 479 us; the launch traced here: 478 us
  waiting for transfers between devices  388 us (81%)
  matrix products  69.2 us (14%)
  between operations  13.4 us (3%)
  local copies, waits for them, and re-layouts  7.04 us (1%)
    reduce_scatter x1, waiting for transfers between devices, on_device(): return lax.psum_scatter(total, 'feat', scatter_dimension=0, tiled=True)  246 us
    ppermute x15, waiting for transfers between devices, shifted(): return lax.ppermute(block, axis, route)  143 us
    dot_general x16, matrix products, block_scores(): lax.dot_general(block, train_grads, (((1,), (1,)), ((), ())), preferred_e...  69.2 us
  transfers between devices with their start and end apart: 16, of which 16 were waited for; matrix products, arithmetic and copies ran while one was open for 0% of the time, Pallas kernels for 0%

commit v1 on v0

v1 whole, which is shorter than its diff:
```python
import jax
import jax.numpy as jnp
from jax import lax
from jax.sharding import Mesh
from jax.sharding import PartitionSpec as P

EX = ("y", "xl", "c")
FEAT = ("xh", "z")


def on_device(queries, train_grads):
    everyone = lax.all_gather(queries, EX, tiled=True)
    part = lax.dot_general(
        everyone, train_grads, (((1,), (1,)), ((), ())), preferred_element_type=jnp.float32
    )
    rows = queries.shape[0]
    part = part.reshape(2, 8 * rows, train_grads.shape[0])
    part = lax.psum_scatter(part, "z", scatter_dimension=1, tiled=True)
    return lax.psum_scatter(part, "xh", scatter_dimension=0, tiled=False)


def solution(mesh):
    fine = Mesh(mesh.devices.reshape(2, 8, 4, 2, 2), FEAT + EX)
    return jax.shard_map(
        on_device,
        mesh=fine,
        in_specs=(P(EX, FEAT), P(EX, FEAT)),
        out_specs=P(FEAT, EX),
        check_vma=False,
    )
```

time: 479 us -> 213 us (0.44)
  waiting for transfers between devices: 388 us -> 184 us
  matrix products: 69.2 us -> 14.5 us
  local copies, waits for them, and re-layouts: 7.04 us -> 0 us
    ppermute x15 -> x0, waiting for transfers between devices: 143 us -> none  [shifted(): return lax.ppermute(block, axis, route)]
    reduce_scatter x1 -> x2, waiting for transfers between devices: 246 us -> 124 us  [the longest x1 96 us: on_device(): part = lax.psum_scatter(part, 'z', scatter_dimension=1, tiled=True)]
    all_gather x0 -> x1, waiting for transfers between devices: none -> 59.5 us  [on_device(): everyone = lax.all_gather(queries, EX, tiled=True)]
    dot_general x16 -> x1, matrix products: 69.2 us -> 14.5 us  [on_device(): lax.dot_general(everyone, train_grads, (((1,), (1,)), ((), ())), preferre...]
    unnamed x5 -> x0, local copies, waits for them, and re-layouts: 5.38 us -> none
  transfers between devices with their start and end apart: 16 -> 3, of which waited for: 16 -> 3; matrix products, arithmetic and copies ran while one was open for 0% -> 0% of each run, Pallas kernels for 0% -> 0%
where the time goes in v1:
time: 213 us; the launch traced here: 212 us
  waiting for transfers between devices  184 us (86%)
  matrix products  14.5 us (7%)
  between operations  13.1 us (6%)
    reduce_scatter x1, waiting for transfers between devices, on_device(): part = lax.psum_scatter(part, 'z', scatter_dimension=1, tiled=True)  96 us
    all_gather x1, waiting for transfers between devices, on_device(): everyone = lax.all_gather(queries, EX, tiled=True)  59.5 us
    reduce_scatter x1, waiting for transfers between devices, on_device(): return lax.psum_scatter(part, 'xh', scatter_dimension=0, tiled=False)  28 us
    dot_general x1, matrix products, on_device(): lax.dot_general(everyone, train_grads, (((1,), (1,)), ((), ())), preferre...  14.5 us
  transfers between devices with their start and end apart: 3, of which 3 were waited for; matrix products, arithmetic and copies ran while one was open for 0% of the time, Pallas kernels for 0%

profile of v1, /device:TPU:8, one launch (start us, length us, event | category | flops | bytes accessed | tf_op | source)
XLA Modules:
  0.0 212.0 jit_solution(17793294917892226893)
XLA Ops:
  6.5 0.0 all-gather.2.cloned.1.call-start
  6.5 0.7 all-gather.2.cloned.1.call-update
  7.3 0.0 reduce-scatter.3.cloned.1.call-start
  7.3 59.5 %all-gather.2.cloned.1.call-done = bf16[2048,2048]{1,0:T(8,128)(2,1)} async-done(((bf16[128,2048]{1,0:T(8,128)(2,1)}), bf16[2048,2048]{1,0:T(8,128)(2,1)}) %all-gather.2.cloned.1.call-update) | async-done | bytes 8388624 | tf_op jit(solution)/shard_map/all_gather | solution.py:12
  66.8 14.5 %fusion = f32[2048,1024]{1,0:T(8,128)} fusion(bf16[2048,2048]{1,0:T(8,128)(2,1)} %all-gather.2.cloned.1.call-done, bf16[1024,2048]{1,0:T(8,128)(2,1)} %param.3), kind=kOutput, calls=%fused_computation | convolution fusion | flops 8589934592 | bytes 20971520 | tf_op jit(solution)/shard_map/dot_general | solution.py:13
  81.3 0.0 reduce-scatter.3.cloned.1.call-update
  81.3 0.0 reduce-scatter.5.cloned.1.call-start
  81.4 96.0 %reduce-scatter.3.cloned.1.call-done = f32[2,128,1024]{2,1,0:T(8,128)} async-done(((f32[2,1024,1024]{2,1,0:T(8,128)}), f32[2,128,1024]{2,1,0:T(8,128)}) %reduce-scatter.3.cloned.1.call-update) | async-done | bytes 1048592 | tf_op jit(solution)/shard_map/reduce_scatter | solution.py:18
  177.4 0.0 reduce-scatter.5.cloned.1.call-update
  177.4 28.0 %reduce-scatter.5.cloned.1.call-done = f32[1,128,1024]{2,1,0:T(8,128)} async-done(((f32[2,128,1024]{2,1,0:T(8,128)}), f32[1,128,1024]{2,1,0:T(8,128)}) %reduce-scatter.5.cloned.1.call-update) | async-done | bytes 524304 | tf_op jit(solution)/shard_map/reduce_scatter | solution.py:19
Async XLA Ops:
  6.5 60.2 %all-gather.2.cloned.1.call-start = ((), (), s32[]{:S(2)}) async-start(), calls=%async_computation.2 | async-start | bytes 8912896 | tf_op jit(solution)/shard_map/all_gather | solution.py:12
  7.3 170.1 %reduce-scatter.3.cloned.1.call-start = ((), (), s32[]{:S(2)}) async-start(), calls=%async_computation.3 | async-start | bytes 9437184 | tf_op jit(solution)/shard_map/reduce_scatter | solution.py:18
  81.3 124.1 %reduce-scatter.5.cloned.1.call-start = ((), (), s32[]{:S(2)}) async-start(), calls=%async_computation.4 | async-start | bytes 1572864 | tf_op jit(solution)/shard_map/reduce_scatter | solution.py:19
Sparse Core Ops, SparseCore 0:
  9.2 57.5 all-gather.1
  81.4 95.8 reduce-scatter.2
  179.9 25.5 reduce-scatter.4
